TPU v7x, 256 devices: a whole 4x4x8 slice. The times are simulated.
256 devices in a mesh: section: 8 (over z), dp: 8 (over y, core), vocab: 4 (over x).
Axes of the slice: x: 4, y: 4, z: 8, core: 2. Of those that a mesh axis runs over, the one named last changes fastest.
Arguments:
- tokens_in: int32 [32], replicated, may hold values from 0 to 65535
- picks: int32 [1, 32], replicated, may hold values from 0 to 65535
- parents: int32 [1, 32], replicated, may hold values from 0 to 7
- scores: float32 [32], replicated, may hold values from -4 to 4
- embed: bfloat16 [65536, 4096], P('section', ('dp', 'vocab')), may hold values from -6 to 6
- norm_gain: float32 [8, 4096], P('section', ('dp', 'vocab')), may hold values from 0.5 to 1.5
- in_weight: bfloat16 [8, 4096, 2, 4096], P('section', ('dp', 'vocab')), may hold values from -0.09375 to 0.09375
- conv_weight: float32 [8, 4, 4096], P('section', None, 'vocab'), may hold values from -3 to 3
- conv_bias: float32 [8, 4096], P('section', 'vocab'), may hold values from -3 to 3
- xdt_weight: bfloat16 [8, 4096, 256], P('section', 'vocab'), may hold values from -0.09375 to 0.09375
- xbc_weight: bfloat16 [8, 4096, 32], P('section', 'vocab'), may hold values from -0.09375 to 0.09375
- dt_weight: bfloat16 [8, 256, 4096], P('section', None, 'vocab'), may hold values from -0.375 to 0.375
- dt_bias: float32 [8, 4096], P('section', 'vocab'), may hold values from -4 to -1
- a_rate: float32 [8, 16, 4096], P('section', None, 'vocab'), may hold values from 0.5 to 16
- skip: float32 [8, 4096], P('section', 'vocab'), may hold values from 0.1 to 1.9
- out_weight: bfloat16 [8, 4096, 4096], P('section', None, ('dp', 'vocab')), may hold values from -0.09375 to 0.09375
- final_gain: float32 [4096], replicated, may hold values from 0.5 to 1.5
- head: bfloat16 [65536, 4096], P(('section', 'dp', 'vocab'))
- conv_state: bfloat16 [8, 32, 3, 4096], P('section', 'dp', None, 'vocab'), may hold values from -6 to 6
- ssm_state: float32 [8, 32, 16, 4096], P('section', 'dp', None, 'vocab'), may hold values from -6 to 6
Outputs:
- conv_out: bfloat16 [8, 32, 3, 4096], P('section', 'dp', None, 'vocab')
- ssm_out: float32 [8, 32, 16, 4096], P('section', 'dp', None, 'vocab')
- final_scores: float32 [32], replicated
Inputs may be any that keep to these rules, and one draw needn't show every extreme that they name: parents[k, g] is a beam number of the source of row g.
All inputs are finite; a program needn't handle non-finite values.
Results may differ from a plain program's by a relative error of at most 0.015.
Values may be sent and summed in bfloat16 or wider, within the bound.
No kernel may reach another device: no remote copies, remote signals or barrier semaphores. Data moves between devices by JAX's collectives and lax.ppermute only.
A program may use at most 128 MiB of HBM per device.

v0:
```python
import jax
import jax.numpy as jnp
from jax import lax
from jax.experimental import pallas as pl
from jax.experimental.pallas import tpu as pltpu
from jax.sharding import PartitionSpec as P

STATE_DIM = 16
SOURCES = 4
EPSILON = 1e-05
TAIL = 128
PAD = 8

F32 = jnp.float32
BF16 = jnp.bfloat16


def by_vocab(value, by):
    n = lax.axis_size("vocab")
    return lax.ppermute(value, "vocab", [(i, (i + by) % n) for i in range(n)])


def by_y(value, by):
    n = lax.axis_size("dp") // 2
    pairs = [(2 * y + c, 2 * ((y + by) % n) + c) for y in range(n) for c in range(2)]
    return lax.ppermute(value, "dp", pairs)


def over_side(value):
    n = lax.axis_size("dp") // 2
    m = lax.axis_size("vocab")
    groups = [[(2 * y + c) * m + v for y in range(n) for v in range(m)] for c in range(2)]
    return lax.all_to_all(value, ("dp", "vocab"), 0, 0, tiled=True, axis_index_groups=groups)


def other_core(value):
    n = lax.axis_size("dp")
    return lax.ppermute(value, "dp", [(i, i ^ 1) for i in range(n)])


def next_section(value):
    n = lax.axis_size("section")
    return lax.ppermute(value, "section", [(i, (i + 1) % n) for i in range(n)])


def whole(space=pltpu.VMEM):
    return pl.BlockSpec(memory_space=space)


def place_rows(groups, at_ref, own_ref, oth_ref, hidden_ref, gain_ref):
    rows, block = own_ref.shape[1:]
    for half, ref in enumerate((own_ref, oth_ref)):
        columns = slice(half * block, (half + 1) * block)
        gain_ref[:, columns] = ref[groups, 0:1, :]
        for y in range(groups // 2):
            hidden_ref[y * rows : (y + 1) * rows, columns] = ref[2 * y + at_ref[1]]


def choose_rows(at_ref, parent_ref, own_ref, oth_ref, o0, o1, o2, o3):
    rows = own_ref.shape[0]
    y, c = at_ref[0], at_ref[1]
    for k, out in enumerate((o0, o1, o2, o3)):
        beam = 2 * lax.rem(y + 4 - k, 4) + c
        for r in range(rows):
            own = lax.rem(parent_ref[beam * rows + r], 2) == c
            picked = jnp.where(own, own_ref[r].astype(F32), oth_ref[r].astype(F32))
            out[r] = picked.astype(BF16)


def settle_rows(at_ref, parent_ref, s0, s1, s2, s3, ssm_ref, conv_ref):
    rows = s0.shape[0]
    y, c = at_ref[0], at_ref[1]
    for r in range(rows):
        parent = parent_ref[(2 * y + c) * rows + r]
        slot = lax.rem(lax.div(parent, 2) + 4 - y, 4)
        row = s0[r].astype(F32)
        for k, ref in ((1, s1), (2, s2), (3, s3)):
            row = jnp.where(slot == k, ref[r].astype(F32), row)
        ssm_ref[r] = row[:STATE_DIM]
        conv_ref[r] = row[STATE_DIM:].astype(BF16)


def project_in(columns, h_ref, gain_ref, w_ref, out_ref, scr):
    wide = w_ref.shape[1]
    rows = out_ref.shape[1]
    sides = 4
    chan = (out_ref.shape[2] - TAIL) // (sides + 1)
    hidden = h_ref[...]
    normed = (hidden * gain_ref[...]).astype(BF16)
    squares = jnp.sum(hidden * hidden, axis=1, keepdims=True)
    high = squares.astype(BF16).astype(F32)
    lane = lax.broadcasted_iota(jnp.int32, (hidden.shape[0], TAIL), 1)
    scr[:, wide:] = jnp.where(lane == 0, high, jnp.where(lane == 1, squares - high, 0.0))
    for at in range(0, wide, columns):
        there = slice(at, at + columns)
        scr[:, there] = jnp.dot(normed, w_ref[:, there], preferred_element_type=F32)
    for y in range(out_ref.shape[0] // sides):
        own = slice(y * rows, (y + 1) * rows)
        for v in range(sides):
            place = y * sides + v
            for j in range(sides):
                at = ((v - j) % sides) * chan
                out_ref[place, :, j * chan : (j + 1) * chan] = scr[own, at : at + chan].astype(BF16)
            at = (sides + v) * chan
            there = slice(sides * chan, (sides + 1) * chan)
            out_ref[place, :, there] = scr[own, at : at + chan].astype(BF16)
            out_ref[place, :, (sides + 1) * chan :] = scr[own, wide:].astype(BF16)


def advance(
    section, model_width, at_ref, sums_ref, small_ref, c1, c2, c3, x0, x1, x2, x3, w_dt, x_in, ssm_in,
    mixed_ref, x_out, ssm_out, scr,
):
    total = sums_ref[0].astype(F32)
    for i in range(1, sums_ref.shape[0]):
        total = total + sums_ref[i].astype(F32)
    rows = total.shape[0]
    chan = w_dt.shape[1]
    wide = total.shape[1] - TAIL
    squares = total[:, wide : wide + 1] + total[:, wide + 1 : wide + 2]
    scale = lax.rsqrt(squares / model_width + EPSILON)
    projected = (total[:, :wide] * scale).astype(BF16).astype(F32)
    acts = []
    terms = jnp.zeros((rows, x0.shape[1]), F32)
    for j, (conv, w) in enumerate(zip((small_ref, c1, c2, c3), (x0, x1, x2, x3))):
        x = projected[:, j * chan : (j + 1) * chan]
        acts.append(jax.nn.silu(conv[0:rows, :] + x * conv[rows : rows + 1, :]))
        terms = terms + jnp.dot(acts[j].astype(BF16), w[...], preferred_element_type=F32)
    act = acts[0]
    gate = jax.nn.silu(projected[:, wide - chan :])
    rank = w_dt.shape[0]
    low = terms[:, :rank].astype(BF16)
    pre = jnp.dot(low, w_dt[...], preferred_element_type=F32)
    pre = pre + small_ref[rows + 1 : rows + 2, :]
    step = jnp.maximum(pre, 0.0) + jnp.log1p(jnp.exp(-jnp.abs(pre)))
    scr[0] = step
    scr[1] = step * act
    bc = terms[:, rank : rank + 2 * STATE_DIM]
    shape = (STATE_DIM, 2 * STATE_DIM)
    lane = lax.broadcasted_iota(jnp.int32, shape, 1)
    sub = lax.broadcasted_iota(jnp.int32, shape, 0)
    rates = small_ref[PAD:, :]
    live = at_ref[3] == section
    for g in range(rows):
        line = jnp.broadcast_to(bc[g : g + 1, :], shape)
        b_col = jnp.sum(jnp.where(lane == sub, line, 0.0), axis=1, keepdims=True)
        c_col = jnp.sum(jnp.where(lane == sub + STATE_DIM, line, 0.0), axis=1, keepdims=True)
        old = ssm_in[g]
        new = jnp.exp(-scr[0, g : g + 1, :] * rates) * old + b_col * scr[1, g : g + 1, :]
        scr[2, g : g + 1, :] = jnp.sum(c_col * new, axis=0, keepdims=True)
        ssm_out[g] = jnp.where(live, new, old)
    x_out[...] = jnp.where(live, projected[:, :chan], x_in[...])
    mixed = (scr[2] + small_ref[rows + 2 : rows + 3, :] * act) * gate
    mixed = mixed.astype(BF16)
    for i in range(mixed_ref.shape[0]):
        mixed_ref[i] = mixed


def project_out(sides, m_ref, h_ref, w_ref, out_ref, scr):
    rows, chan = m_ref.shape[1:]
    total = h_ref[...]
    for v in range(sides):
        for y in range(m_ref.shape[0] // sides):
            scr[y * rows : (y + 1) * rows, :] = m_ref[y * sides + v].astype(F32)
        total = total + jnp.dot(
            scr[...].astype(BF16),
            w_ref[v * chan : (v + 1) * chan, :],
            preferred_element_type=F32,
        )
    out_ref[...] = total


def finish(at_ref, h_ref, gain_ref, out_ref):
    rows = h_ref[...]
    width = rows.shape[1]
    half = width // 2
    first = at_ref[1] == 0
    left = jnp.where(first, rows[:, :half], rows[:, half:])
    right = jnp.where(first, rows[:, half:], rows[:, :half])
    out_ref[:, :half] = (left * gain_ref[:, :half]).astype(BF16)
    out_ref[:, half:width] = (right * gain_ref[:, half:]).astype(BF16)
    squares = jnp.sum(rows * rows, axis=1, keepdims=True)
    high = squares.astype(BF16).astype(F32)
    lane = lax.broadcasted_iota(jnp.int32, (rows.shape[0], TAIL), 1)
    tail = jnp.where(lane == 0, high, jnp.where(lane == 1, squares - high, 0.0))
    out_ref[:, width:] = tail.astype(BF16)


def local_call(body, outs, scratch=(), smem=0, operands=0, aliases=None, cost=None):
    specs = [whole(pltpu.SMEM)] * smem + [whole()] * (operands - smem)
    return pl.pallas_call(
        body,
        out_shape=[jax.ShapeDtypeStruct(shape, dtype) for shape, dtype in outs],
        in_specs=specs,
        out_specs=[whole()] * len(outs),
        scratch_shapes=[pltpu.VMEM(shape, F32) for shape in scratch],
        input_output_aliases=aliases or {},
        compiler_params=pltpu.CompilerParams(vmem_limit_bytes=12 * 2**20),
        cost_estimate=cost,
    )


def on_device(
    tokens_in,
    picks,
    parents,
    scores,
    embed,
    norm_gain,
    in_weight,
    conv_weight,
    conv_bias,
    xdt_weight,
    xbc_weight,
    dt_weight,
    dt_bias,
    a_rate,
    skip,
    out_weight,
    final_gain,
    head,
    conv_state,
    ssm_state,
):
    section_count = lax.axis_size("section")
    dp_count = lax.axis_size("dp")
    vocab_count = lax.axis_size("vocab")
    y_count = dp_count // 2
    row_total = tokens_in.shape[0]
    own_rows = row_total // dp_count
    core_rows = own_rows * y_count
    section_at = lax.axis_index("section")
    dp_at = lax.axis_index("dp")
    vocab_at = lax.axis_index("vocab")
    y_at = dp_at // 2
    core_at = dp_at % 2
    block = in_weight.shape[1]
    chan = in_weight.shape[3] // vocab_count
    model_width = final_gain.shape[0]
    pair_width = 2 * block
    sides = y_count * vocab_count
    vocab_rows = head.shape[0]

    coords = jnp.stack([y_at, core_at, vocab_at, section_at]).astype(jnp.int32)

    embed_rows = embed.shape[0]
    local_ids = tokens_in - section_at * embed_rows
    inside = (local_ids >= 0) & (local_ids < embed_rows)
    found = jnp.take(embed, jnp.clip(local_ids, 0, embed_rows - 1), axis=0)
    found = jnp.where(inside[:, None], found, 0).astype(BF16)
    found, in_own, ssm_now = lax.optimization_barrier((found, in_weight[0], ssm_state[0]))
    copies = jnp.broadcast_to(found[None], (section_count,) + found.shape)
    pieces = lax.all_to_all(copies, "section", 0, 0, tiled=True)
    looked_up = jnp.sum(pieces.astype(F32), axis=0).reshape(dp_count, own_rows, block)
    beside = jnp.pad(norm_gain, ((0, own_rows - 1), (0, 0)))
    bundle = jnp.concatenate([looked_up, beside[None]], axis=0)
    hidden, gain = local_call(
        lambda *refs: place_rows(dp_count, *refs),
        [((core_rows, pair_width), F32), ((1, pair_width), F32)],
        smem=1,
        operands=3,
    )(coords, bundle, other_core(bundle))

    in_own = in_own.reshape(block, 2 * vocab_count * chan)
    w_in = jnp.concatenate([in_own, other_core(in_own)], axis=0)
    w_out = jnp.concatenate([out_weight[0], other_core(out_weight[0])], axis=1)

    w_x = jnp.concatenate([xdt_weight[0], xbc_weight[0]], axis=1)
    w_dt = dt_weight[0]
    taps = conv_weight[0]
    conv_old = conv_state[0]
    keep = taps.shape[0] - 1
    conv_pre = conv_bias + jnp.sum(conv_old.astype(F32) * taps[None, :keep], axis=1)
    small = jnp.concatenate(
        [conv_pre, taps[keep:], dt_bias, skip, jnp.zeros((1, chan), F32), a_rate[0]], axis=0
    )
    x_kept = jnp.zeros((own_rows, chan), F32)

    wide = (vocab_count + 1) * chan + TAIL
    _, w_x = lax.optimization_barrier((found, w_x))
    all_x = [w_x] + [by_vocab(w_x, k) for k in range(1, vocab_count)]
    all_conv = [by_vocab(small[:PAD], k) for k in range(1, vocab_count)]
    call_in = local_call(
        lambda *refs: project_in(512, *refs),
        [((sides, own_rows, wide), BF16)],
        scratch=[(core_rows, 2 * vocab_count * chan + TAIL)],
        operands=3,
        cost=pl.CostEstimate(
            flops=4 * core_rows * pair_width * vocab_count * chan,
            bytes_accessed=4 * pair_width * vocab_count * chan,
            transcendentals=0,
        ),
    )
    def call_state(section, *operands):
        return local_call(
            lambda *refs: advance(section, model_width, *refs),
            [((sides, own_rows, chan), BF16), ((own_rows, chan), F32), (ssm_now.shape, F32)],
            scratch=[(3, own_rows, chan)],
            smem=1,
            operands=13,
            aliases={11: 1, 12: 2},
            cost=pl.CostEstimate(
                flops=10 * own_rows * chan * dt_weight.shape[1],
                bytes_accessed=10 * chan * dt_weight.shape[1] + 8 * ssm_now.size,
                transcendentals=ssm_now.size,
            ),
        )(*operands)

    call_out = local_call(
        lambda *refs: project_out(vocab_count, *refs),
        [((core_rows, pair_width), F32)],
        scratch=[(core_rows, chan)],
        operands=3,
        cost=pl.CostEstimate(
            flops=2 * core_rows * pair_width * vocab_count * chan,
            bytes_accessed=2 * pair_width * vocab_count * chan,
            transcendentals=0,
        ),
    )

    for step in range(section_count):
        (parts,) = call_in(hidden, gain, w_in)
        if step == 0:
            _, all_x, w_out = lax.optimization_barrier((parts, all_x, w_out))
        mixed, x_kept, ssm_now = call_state(
            step, coords, over_side(parts), small, *all_conv, *all_x, w_dt, x_kept, ssm_now
        )
        (hidden,) = call_out(over_side(mixed), hidden, w_out)
        if step + 1 < section_count:
            hidden = next_section(hidden)

    pair_gain = final_gain.reshape(y_count, 2, vocab_count, block)
    pair_gain = lax.dynamic_index_in_dim(pair_gain, y_at, 0, keepdims=False)
    pair_gain = lax.dynamic_index_in_dim(pair_gain, vocab_at, 1, keepdims=False)
    (sent,) = local_call(
        finish,
        [((core_rows, pair_width + TAIL), BF16)],
        smem=1,
        operands=3,
    )(coords, hidden, pair_gain.reshape(1, pair_width))
    last = section_count - 1
    middle = last // 2
    got = lax.ppermute(sent, "section", [(last, middle)])
    sent = jnp.where(section_at == middle, got, sent)
    received = jnp.zeros_like(sent)
    for k in range(1, middle + 1):
        pairs = [(last, (last + k) % section_count), (middle, middle + k)]
        received = received + lax.ppermute(sent, "section", pairs)
    _, ssm_now, x_kept = lax.optimization_barrier((got, ssm_now, x_kept))
    conv_next = jnp.concatenate([conv_old[:, 1:], x_kept.astype(BF16)[:, None]], axis=1)
    states = jnp.concatenate([ssm_now.astype(BF16), conv_next], axis=1)
    chosen = local_call(
        choose_rows,
        [(states.shape, BF16)] * y_count,
        smem=2,
        operands=4,
    )(coords, parents[0], states, other_core(states))
    chosen = [chosen[0]] + [by_y(chosen[k], -k) for k in range(1, y_count)]
    ssm_new, conv_new = local_call(
        settle_rows,
        [(ssm_now.shape, F32), (conv_next.shape, BF16)],
        smem=2,
        operands=6,
    )(coords, parents[0], *chosen)
    is_source = (section_at == middle) | (section_at == last)
    sent = jnp.where(is_source, sent, received)
    every = over_side(jnp.broadcast_to(sent[None], (sides,) + sent.shape))
    facing = other_core(every)
    cores = jnp.where(core_at == 0, jnp.stack([every, facing]), jnp.stack([facing, every]))
    cores = cores.reshape(2, y_count, vocab_count, y_count, own_rows, pair_width + TAIL)
    sums = jnp.sum(cores[..., pair_width : pair_width + 2].astype(F32), axis=(1, 2, 5))
    sums = jnp.transpose(sums, (1, 0, 2)).reshape(row_total)
    final = cores[..., :pair_width].reshape(2, y_count, vocab_count, y_count, own_rows, 2, block)
    final = jnp.transpose(final, (3, 0, 4, 1, 5, 2, 6)).reshape(row_total, model_width)
    final_scale = lax.rsqrt(sums / model_width + EPSILON)
    logits = lax.dot_general(final, head, (((1,), (1,)), ((), ())), preferred_element_type=F32)
    logits = logits * final_scale[:, None]

    source_of = jnp.arange(row_total, dtype=jnp.int32) % SOURCES
    parent_row = parents[0] * SOURCES + source_of
    vocab_offset = lax.axis_index(("section", "dp", "vocab")) * vocab_rows
    parent_logits = jnp.take(logits, parent_row, axis=0)
    is_pick = jnp.arange(vocab_rows, dtype=jnp.int32)[None, :] + vocab_offset == picks[0][:, None]
    picked = jnp.sum(jnp.where(is_pick, parent_logits, 0.0), axis=1)
    top = jnp.max(logits, axis=1)
    total = jnp.sum(jnp.exp(logits - top[:, None]), axis=1)
    for axes in (("dp", "vocab"), ("section",)):
        stats = jnp.stack([top, total, picked] + [jnp.zeros_like(top)] * 5)
        stats = jnp.pad(stats, ((0, 0), (0, 128 - row_total)))
        copies = jnp.broadcast_to(stats[None], (lax.axis_size(axes),) + stats.shape)
        every = lax.all_to_all(copies, axes, 0, 0, tiled=True)[:, :, :row_total]
        tops, totals, picks_of = every[:, 0], every[:, 1], every[:, 2]
        top = jnp.max(tops, axis=0)
        total = jnp.sum(totals * jnp.exp(tops - top[None]), axis=0)
        picked = jnp.sum(picks_of, axis=0)
    log_norm = top + jnp.log(total)
    scores_now = jnp.take(scores, parent_row) + picked - jnp.take(log_norm, parent_row)

    return (conv_new[None], ssm_new[None], scores_now)


def solution(mesh):
    placed = (
        P(),
        P(),
        P(),
        P(),
        P("section", ("dp", "vocab")),
        P("section", ("dp", "vocab")),
        P("section", ("dp", "vocab"), None, None),
        P("section", None, "vocab"),
        P("section", "vocab"),
        P("section", "vocab", None),
        P("section", "vocab", None),
        P("section", None, "vocab"),
        P("section", "vocab"),
        P("section", None, "vocab"),
        P("section", "vocab"),
        P("section", None, ("dp", "vocab")),
        P(),
        P(("section", "dp", "vocab"), None),
        P("section", "dp", None, "vocab"),
        P("section", "dp", None, "vocab"),
    )
    return jax.shard_map(
        on_device,
        mesh=mesh,
        in_specs=placed,
        out_specs=(P("section", "dp", None, "vocab"), P("section", "dp", None, "vocab"), P()),
        check_vma=False,
    )
```

profile of v0, /device:TPU:1, one launch (start us, length us, event | category | flops | bytes accessed | tf_op | source)
XLA Modules:
  0.0 394.2 jit_solution(6933808565067875921)
XLA Ops:
  7.4 4.2 %copy.164 = bf16[16,8,2,4096]{3,1,2,0:T(8,128)(2,1)} copy(bf16[16,8,2,4096]{3,2,1,0:T(2,128)(2,1)} %bitcast.79) | data formatting | bytes 4194304
  21.0 8.2 %all-to-all-start = ((bf16[8,32,128]{2,1,0:T(8,128)(2,1)}), bf16[8,32,128]{2,1,0:T(8,128)(2,1)S(1)}, u32[]{:S(2)}, u32[]{:S(2)}) async-start(bf16[8,32,128]{2,1,0:T(8,128)(2,1)} %broadcast_in_dim.98), calls=%async_computation | async-start | bytes 131072 | tf_op jit(solution)/shard_map/all_to_all | solution.py:253
  47.5 4.4 %all-to-all-start.1 = ((bf16[16,4,5248]{2,1,0:T(4,128)(2,1)}), bf16[16,4,5248]{2,1,0:T(4,128)(2,1)}, u32[]{:S(2)}, u32[]{:S(2)}) async-start(bf16[16,4,5248]{2,1,0:T(4,128)(2,1)} %shard_map.212), calls=%async_computation.1 | async-start | bytes 1343488 | tf_op jit(solution)/shard_map/all_to_all | solution.py:33
  75.0 11.0 %all_to_all.100.refs_0_ = bf16[16,4,1024]{2,1,0:T(4,128)(2,1)S(1)} all-to-all(bf16[16,4,1024]{2,1,0:T(4,128)(2,1)S(1)} %get-tuple-element.57), channel_id=1, replica_groups={{0,1,2,3,8,9,10,11,16,17,18,19,24,25,26,27},{4,5,6,7,12,13,14,15,20,21,..., dimensions={0} | all-to-all | bytes 262144 | tf_op jit(solution)/shard_map/all_to_all | solution.py:33
  92.5 13.0 %all_to_all.101.refs_1_ = bf16[16,4,5248]{2,1,0:T(4,128)(2,1)S(1)} all-to-all(bf16[16,4,5248]{2,1,0:T(4,128)(2,1)S(1)} %shard_map.215), channel_id=1, replica_groups={{0,1,2,3,8,9,10,11,16,17,18,19,24,25,26,27},{4,5,6,7,12,13,14,15,20,21,..., dimensions={0} | all-to-all | bytes 1343488 | tf_op jit(solution)/shard_map/all_to_all | solution.py:33
  107.6 9.8 %all_to_all.102.refs_0_ = bf16[16,4,1024]{2,1,0:T(4,128)(2,1)S(1)} all-to-all(bf16[16,4,1024]{2,1,0:T(4,128)(2,1)S(1)} %get-tuple-element.61), channel_id=1, replica_groups={{0,1,2,3,8,9,10,11,16,17,18,19,24,25,26,27},{4,5,6,7,12,13,14,15,20,21,..., dimensions={0} | all-to-all | bytes 262144 | tf_op jit(solution)/shard_map/all_to_all | solution.py:33
  117.9 4.1 %collective-permute-done.10.refs_0_.refs_1_ = f32[16,256]{1,0:T(8,128)S(1)} collective-permute-done((f32[16,256]{1,0:T(8,128)S(1)}, f32[16,256]{1,0:T(8,128)S(1)}, u32[]{:S(2)}, u32[]{:S(2)}) %collective-permute-start.10) | collective-permute-done | bytes 16416 | tf_op jit(solution)/shard_map/ppermute | solution.py:43
  122.6 12.6 %all_to_all.103.refs_1_ = bf16[16,4,5248]{2,1,0:T(4,128)(2,1)S(1)} all-to-all(bf16[16,4,5248]{2,1,0:T(4,128)(2,1)S(1)} %shard_map.218), channel_id=1, replica_groups={{0,1,2,3,8,9,10,11,16,17,18,19,24,25,26,27},{4,5,6,7,12,13,14,15,20,21,..., dimensions={0} | all-to-all | bytes 1343488 | tf_op jit(solution)/shard_map/all_to_all | solution.py:33
  137.2 9.6 %all_to_all.104.refs_0_ = bf16[16,4,1024]{2,1,0:T(4,128)(2,1)S(1)} all-to-all(bf16[16,4,1024]{2,1,0:T(4,128)(2,1)S(1)} %get-tuple-element.64), channel_id=1, replica_groups={{0,1,2,3,8,9,10,11,16,17,18,19,24,25,26,27},{4,5,6,7,12,13,14,15,20,21,..., dimensions={0} | all-to-all | bytes 262144 | tf_op jit(solution)/shard_map/all_to_all | solution.py:33
  151.7 12.6 %all_to_all.105.refs_1_ = bf16[16,4,5248]{2,1,0:T(4,128)(2,1)S(1)} all-to-all(bf16[16,4,5248]{2,1,0:T(4,128)(2,1)S(1)} %shard_map.221), channel_id=1, replica_groups={{0,1,2,3,8,9,10,11,16,17,18,19,24,25,26,27},{4,5,6,7,12,13,14,15,20,21,..., dimensions={0} | all-to-all | bytes 1343488 | tf_op jit(solution)/shard_map/all_to_all | solution.py:33
  166.3 10.4 %all_to_all.106.refs_0_ = bf16[16,4,1024]{2,1,0:T(4,128)(2,1)S(1)} all-to-all(bf16[16,4,1024]{2,1,0:T(4,128)(2,1)S(1)} %get-tuple-element.67), channel_id=1, replica_groups={{0,1,2,3,8,9,10,11,16,17,18,19,24,25,26,27},{4,5,6,7,12,13,14,15,20,21,..., dimensions={0} | all-to-all | bytes 262144 | tf_op jit(solution)/shard_map/all_to_all | solution.py:33
  181.5 12.5 %all_to_all.107.refs_1_ = bf16[16,4,5248]{2,1,0:T(4,128)(2,1)S(1)} all-to-all(bf16[16,4,5248]{2,1,0:T(4,128)(2,1)S(1)} %shard_map.224), channel_id=1, replica_groups={{0,1,2,3,8,9,10,11,16,17,18,19,24,25,26,27},{4,5,6,7,12,13,14,15,20,21,..., dimensions={0} | all-to-all | bytes 1343488 | tf_op jit(solution)/shard_map/all_to_all | solution.py:33
  196.0 9.6 %all_to_all.108.refs_0_ = bf16[16,4,1024]{2,1,0:T(4,128)(2,1)S(1)} all-to-all(bf16[16,4,1024]{2,1,0:T(4,128)(2,1)S(1)} %get-tuple-element.70), channel_id=1, replica_groups={{0,1,2,3,8,9,10,11,16,17,18,19,24,25,26,27},{4,5,6,7,12,13,14,15,20,21,..., dimensions={0} | all-to-all | bytes 262144 | tf_op jit(solution)/shard_map/all_to_all | solution.py:33
  206.1 8.7 %collective-permute-start.13 = (f32[16,256]{1,0:T(8,128)S(1)}, f32[16,256]{1,0:T(8,128)S(1)}, u32[]{:S(2)}, u32[]{:S(2)}) collective-permute-start(f32[16,256]{1,0:T(8,128)S(1)} %shard_map.226), channel_id=1, source_target_pairs={{0,32},{32,64},{64,96},{96,128},{128,160},{160,192},{192,224},{224... | collective-permute-start | bytes 49160 | tf_op jit(solution)/shard_map/ppermute | solution.py:43
  219.3 12.9 %all_to_all.109.refs_1_ = bf16[16,4,5248]{2,1,0:T(4,128)(2,1)S(1)} all-to-all(bf16[16,4,5248]{2,1,0:T(4,128)(2,1)S(1)} %shard_map.227), channel_id=1, replica_groups={{0,1,2,3,8,9,10,11,16,17,18,19,24,25,26,27},{4,5,6,7,12,13,14,15,20,21,..., dimensions={0} | all-to-all | bytes 1343488 | tf_op jit(solution)/shard_map/all_to_all | solution.py:33
  234.1 9.6 %all_to_all.110.refs_0_ = bf16[16,4,1024]{2,1,0:T(4,128)(2,1)S(1)} all-to-all(bf16[16,4,1024]{2,1,0:T(4,128)(2,1)S(1)} %get-tuple-element.73), channel_id=1, replica_groups={{0,1,2,3,8,9,10,11,16,17,18,19,24,25,26,27},{4,5,6,7,12,13,14,15,20,21,..., dimensions={0} | all-to-all | bytes 262144 | tf_op jit(solution)/shard_map/all_to_all | solution.py:33
  248.9 12.5 %all_to_all.111.refs_1_ = bf16[16,4,5248]{2,1,0:T(4,128)(2,1)S(1)} all-to-all(bf16[16,4,5248]{2,1,0:T(4,128)(2,1)S(1)} %shard_map.230), channel_id=1, replica_groups={{0,1,2,3,8,9,10,11,16,17,18,19,24,25,26,27},{4,5,6,7,12,13,14,15,20,21,..., dimensions={0} | all-to-all | bytes 1343488 | tf_op jit(solution)/shard_map/all_to_all | solution.py:33
  263.4 9.6 %all_to_all.112.refs_0_ = bf16[16,4,1024]{2,1,0:T(4,128)(2,1)S(1)} all-to-all(bf16[16,4,1024]{2,1,0:T(4,128)(2,1)S(1)} %get-tuple-element.76), channel_id=1, replica_groups={{0,1,2,3,8,9,10,11,16,17,18,19,24,25,26,27},{4,5,6,7,12,13,14,15,20,21,..., dimensions={0} | all-to-all | bytes 262144 | tf_op jit(solution)/shard_map/all_to_all | solution.py:33
  277.9 12.6 %all_to_all.113.refs_1_ = bf16[16,4,5248]{2,1,0:T(4,128)(2,1)S(1)} all-to-all(bf16[16,4,5248]{2,1,0:T(4,128)(2,1)S(1)} %shard_map.233), channel_id=1, replica_groups={{0,1,2,3,8,9,10,11,16,17,18,19,24,25,26,27},{4,5,6,7,12,13,14,15,20,21,..., dimensions={0} | all-to-all | bytes 1343488 | tf_op jit(solution)/shard_map/all_to_all | solution.py:33
  298.2 6.1 %all-to-all-done.16.refs_0_ = bf16[16,4,1024]{2,1,0:T(4,128)(2,1)S(1)} async-done(((bf16[16,4,1024]{2,1,0:T(4,128)(2,1)}), bf16[16,4,1024]{2,1,0:T(4,128)(2,1)S(1)}, u32[]{:S(2)}, u32[]{:S(2)}) %all-to-all-start.16) | async-done | bytes 131104 | tf_op jit(solution)/shard_map/all_to_all | solution.py:33
  318.5 7.1 %all-to-all-done.17 = bf16[16,16,384]{2,1,0:T(8,128)(2,1)S(1)} async-done(((bf16[16,16,384]{2,1,0:T(8,128)(2,1)}), bf16[16,16,384]{2,1,0:T(8,128)(2,1)S(1)}, u32[]{:S(2)}, u32[]{:S(2)}) %all-to-all-start.17) | async-done | bytes 196640 | tf_op jit(solution)/shard_map/all_to_all | solution.py:33
  325.6 31.4 %collective-permute-start.24 = (bf16[16,16,384]{2,1,0:T(8,128)(2,1)S(1)}, bf16[16,16,384]{2,1,0:T(8,128)(2,1)S(1)}, u32[]{:S(2)}, u32[]{:S(2)}) collective-permute-start(bf16[16,16,384]{2,1,0:T(8,128)(2,1)S(1)} %all-to-all-done.17), channel_id=1, source_target_pairs={{0,4},{4,0},{8,12},{12,8},{16,20},{20,16},{24,28},{28,24},{1,5},{5... | collective-permute-start | bytes 589832 | tf_op jit(solution)/shard_map/ppermute | solution.py:38
  361.8 4.8 %all-to-all-start.18 = ((f32[32,8,128]{2,1,0:T(8,128)}), f32[32,8,128]{2,1,0:T(8,128)}, u32[]{:S(2)}, u32[]{:S(2)}) async-start(f32[32,8,128]{2,1,0:T(8,128)} %broadcast_in_dim.109), calls=%async_computation.18 | async-start | bytes 262144 | tf_op jit(solution)/shard_map/all_to_all | solution.py:391
  376.2 9.5 %all-to-all-start.19 = ((f32[8,8,128]{2,1,0:T(8,128)}), f32[8,8,128]{2,1,0:T(8,128)S(1)}, u32[]{:S(2)}, u32[]{:S(2)}) async-start(f32[8,8,128]{2,1,0:T(8,128)} %broadcast_in_dim.110), calls=%async_computation.19 | async-start | bytes 65536 | tf_op jit(solution)/shard_map/all_to_all | solution.py:391
  (239 shorter events, 145.9 us)
Async XLA Ops:
  11.7 28.9 %collective-permute-start.1 = (bf16[128,8192]{1,0:T(8,128)(2,1)}, bf16[128,8192]{1,0:T(8,128)(2,1)}, u32[]{:S(2)}, u32[]{:S(2)}) collective-permute-start(bf16[128,8192]{1,0:T(8,128)(2,1)} %bitcast.47), channel_id=1, source_target_pairs={{0,4},{4,0},{8,12},{12,8},{16,20},{20,16},{24,28},{28,24},{1,5},{5... | collective-permute-start | bytes 6291464 | tf_op jit(solution)/shard_map/ppermute | solution.py:38
  17.3 36.6 %collective-permute-start.5 = (bf16[1024,288]{0,1:T(8,128)(2,1)}, bf16[1024,288]{0,1:T(8,128)(2,1)}, u32[]{:S(2)}, u32[]{:S(2)}) collective-permute-start(bf16[1024,288]{0,1:T(8,128)(2,1)} %copy.127), channel_id=1, source_target_pairs={{0,1},{1,2},{2,3},{3,0},{4,5},{5,6},{6,7},{7,4},{8,9},{9,10},{10,1... | collective-permute-start | bytes 1769480 | tf_op jit(solution)/shard_map/ppermute | solution.py:20
  17.3 43.5 %collective-permute-start.6 = (bf16[1024,288]{0,1:T(8,128)(2,1)}, bf16[1024,288]{0,1:T(8,128)(2,1)}, u32[]{:S(2)}, u32[]{:S(2)}) collective-permute-start(bf16[1024,288]{0,1:T(8,128)(2,1)} %copy.127), channel_id=1, source_target_pairs={{0,2},{1,3},{2,0},{3,1},{4,6},{5,7},{6,4},{7,5},{8,10},{9,11},{10,... | collective-permute-start | bytes 1769480 | tf_op jit(solution)/shard_map/ppermute | solution.py:20
  19.2 41.5 %collective-permute-start.7 = (bf16[1024,288]{0,1:T(8,128)(2,1)}, bf16[1024,288]{0,1:T(8,128)(2,1)}, u32[]{:S(2)}, u32[]{:S(2)}) collective-permute-start(bf16[1024,288]{0,1:T(8,128)(2,1)} %copy.127), channel_id=1, source_target_pairs={{0,3},{1,0},{2,1},{3,2},{4,7},{5,4},{6,5},{7,6},{8,11},{9,8},{10,9... | collective-permute-start | bytes 1769480 | tf_op jit(solution)/shard_map/ppermute | solution.py:20
  21.0 15.4 %all-to-all-start = ((bf16[8,32,128]{2,1,0:T(8,128)(2,1)}), bf16[8,32,128]{2,1,0:T(8,128)(2,1)S(1)}, u32[]{:S(2)}, u32[]{:S(2)}) async-start(bf16[8,32,128]{2,1,0:T(8,128)(2,1)} %broadcast_in_dim.98), calls=%async_computation | async-start | bytes 131072 | tf_op jit(solution)/shard_map/all_to_all | solution.py:253
  39.6 16.7 %collective-permute-start.8 = (bf16[4096,128]{1,0:T(8,128)(2,1)}, bf16[4096,128]{1,0:T(8,128)(2,1)}, u32[]{:S(2)}, u32[]{:S(2)}) collective-permute-start(bf16[4096,128]{1,0:T(8,128)(2,1)} %bitcast.81), channel_id=1, source_target_pairs={{0,4},{4,0},{8,12},{12,8},{16,20},{20,16},{24,28},{28,24},{1,5},{5... | collective-permute-start | bytes 3145736 | tf_op jit(solution)/shard_map/ppermute | solution.py:38
  47.5 20.1 %all-to-all-start.1 = ((bf16[16,4,5248]{2,1,0:T(4,128)(2,1)}), bf16[16,4,5248]{2,1,0:T(4,128)(2,1)}, u32[]{:S(2)}, u32[]{:S(2)}) async-start(bf16[16,4,5248]{2,1,0:T(4,128)(2,1)} %shard_map.212), calls=%async_computation.1 | async-start | bytes 1343488 | tf_op jit(solution)/shard_map/all_to_all | solution.py:33
  52.5 15.0 %collective-permute-start.2 = (f32[8,1024]{1,0:T(8,128)}, f32[8,1024]{1,0:T(8,128)S(1)}, u32[]{:S(2)}, u32[]{:S(2)}) collective-permute-start(f32[8,1024]{1,0:T(8,128)} %concatenate.26), channel_id=1, source_target_pairs={{0,1},{1,2},{2,3},{3,0},{4,5},{5,6},{6,7},{7,4},{8,9},{9,10},{10,1... | collective-permute-start | bytes 98312 | tf_op jit(solution)/shard_map/ppermute | solution.py:20
  53.9 13.6 %collective-permute-start.3 = (f32[8,1024]{1,0:T(8,128)}, f32[8,1024]{1,0:T(8,128)}, u32[]{:S(2)}, u32[]{:S(2)}) collective-permute-start(f32[8,1024]{1,0:T(8,128)} %concatenate.26), channel_id=1, source_target_pairs={{0,2},{1,3},{2,0},{3,1},{4,6},{5,7},{6,4},{7,5},{8,10},{9,11},{10,... | collective-permute-start | bytes 98312 | tf_op jit(solution)/shard_map/ppermute | solution.py:20
  56.4 11.1 %collective-permute-start.4 = (f32[8,1024]{1,0:T(8,128)}, f32[8,1024]{1,0:T(8,128)}, u32[]{:S(2)}, u32[]{:S(2)}) collective-permute-start(f32[8,1024]{1,0:T(8,128)} %concatenate.26), channel_id=1, source_target_pairs={{0,3},{1,0},{2,1},{3,2},{4,7},{5,4},{6,5},{7,6},{8,11},{9,8},{10,9... | collective-permute-start | bytes 98312 | tf_op jit(solution)/shard_map/ppermute | solution.py:20
  117.9 4.1 %collective-permute-start.10 = (f32[16,256]{1,0:T(8,128)S(1)}, f32[16,256]{1,0:T(8,128)S(1)}, u32[]{:S(2)}, u32[]{:S(2)}) collective-permute-start(f32[16,256]{1,0:T(8,128)S(1)} %shard_map.217), channel_id=1, source_target_pairs={{0,32},{32,64},{64,96},{96,128},{128,160},{160,192},{192,224},{224... | collective-permute-start | bytes 49160 | tf_op jit(solution)/shard_map/ppermute | solution.py:43
  206.1 12.5 %collective-permute-start.13 = (f32[16,256]{1,0:T(8,128)S(1)}, f32[16,256]{1,0:T(8,128)S(1)}, u32[]{:S(2)}, u32[]{:S(2)}) collective-permute-start(f32[16,256]{1,0:T(8,128)S(1)} %shard_map.226), channel_id=1, source_target_pairs={{0,32},{32,64},{64,96},{96,128},{128,160},{160,192},{192,224},{224... | collective-permute-start | bytes 49160 | tf_op jit(solution)/shard_map/ppermute | solution.py:43
  244.1 4.1 %collective-permute-start.14 = (f32[16,256]{1,0:T(8,128)S(1)}, f32[16,256]{1,0:T(8,128)S(1)}, u32[]{:S(2)}, u32[]{:S(2)}) collective-permute-start(f32[16,256]{1,0:T(8,128)S(1)} %shard_map.229), channel_id=1, source_target_pairs={{0,32},{32,64},{64,96},{96,128},{128,160},{160,192},{192,224},{224... | collective-permute-start | bytes 49160 | tf_op jit(solution)/shard_map/ppermute | solution.py:43
  293.8 10.5 %all-to-all-start.16 = ((bf16[16,4,1024]{2,1,0:T(4,128)(2,1)}), bf16[16,4,1024]{2,1,0:T(4,128)(2,1)S(1)}, u32[]{:S(2)}, u32[]{:S(2)}) async-start(bf16[16,4,1024]{2,1,0:T(4,128)(2,1)} %copy-done.16), calls=%async_computation.16 | async-start | bytes 262144 | tf_op jit(solution)/shard_map/all_to_all | solution.py:33
  308.3 5.9 %collective-permute-start.21 = (bf16[16,384]{1,0:T(8,128)(2,1)S(1)}, bf16[16,384]{1,0:T(8,128)(2,1)S(1)}, u32[]{:S(2)}, u32[]{:S(2)}) collective-permute-start(bf16[16,384]{1,0:T(8,128)(2,1)S(1)} %broadcast_select_fusion), channel_id=1, source_target_pairs={{224,0},{96,128},{225,1},{97,129},{226,2},{98,130},{227,3},{99,131... | collective-permute-start | bytes 36872 | tf_op jit(solution)/shard_map/ppermute | solution.py:348
  309.6 4.6 %collective-permute-start.22 = (bf16[16,384]{1,0:T(8,128)(2,1)S(1)}, bf16[16,384]{1,0:T(8,128)(2,1)S(1)}, u32[]{:S(2)}, u32[]{:S(2)}) collective-permute-start(bf16[16,384]{1,0:T(8,128)(2,1)S(1)} %broadcast_select_fusion), channel_id=1, source_target_pairs={{224,32},{96,160},{225,33},{97,161},{226,34},{98,162},{227,35},{99... | collective-permute-start | bytes 36872 | tf_op jit(solution)/shard_map/ppermute | solution.py:348
  315.0 10.7 %all-to-all-start.17 = ((bf16[16,16,384]{2,1,0:T(8,128)(2,1)}), bf16[16,16,384]{2,1,0:T(8,128)(2,1)S(1)}, u32[]{:S(2)}, u32[]{:S(2)}) async-start(bf16[16,16,384]{2,1,0:T(8,128)(2,1)} %broadcast_in_dim.105), calls=%async_computation.17 | async-start | bytes 393216 | tf_op jit(solution)/shard_map/all_to_all | solution.py:33
  325.6 32.5 %collective-permute-start.24 = (bf16[16,16,384]{2,1,0:T(8,128)(2,1)S(1)}, bf16[16,16,384]{2,1,0:T(8,128)(2,1)S(1)}, u32[]{:S(2)}, u32[]{:S(2)}) collective-permute-start(bf16[16,16,384]{2,1,0:T(8,128)(2,1)S(1)} %all-to-all-done.17), channel_id=1, source_target_pairs={{0,4},{4,0},{8,12},{12,8},{16,20},{20,16},{24,28},{28,24},{1,5},{5... | collective-permute-start | bytes 589832 | tf_op jit(solution)/shard_map/ppermute | solution.py:38
  357.1 9.4 %collective-permute-start.17 = (bf16[4,19,1024]{2,1,0:T(8,128)(2,1)S(1)}, bf16[4,19,1024]{2,1,0:T(8,128)(2,1)S(1)}, u32[]{:S(2)}, u32[]{:S(2)}) collective-permute-start(bf16[4,19,1024]{2,1,0:T(8,128)(2,1)S(1)} %pad_maximum_fusion.2.own_ref), channel_id=1, source_target_pairs={{0,4},{4,0},{8,12},{12,8},{16,20},{20,16},{24,28},{28,24},{1,5},{5... | collective-permute-start | bytes 466952 | tf_op jit(solution)/shard_map/ppermute | solution.py:38
  361.8 12.6 %all-to-all-start.18 = ((f32[32,8,128]{2,1,0:T(8,128)}), f32[32,8,128]{2,1,0:T(8,128)}, u32[]{:S(2)}, u32[]{:S(2)}) async-start(f32[32,8,128]{2,1,0:T(8,128)} %broadcast_in_dim.109), calls=%async_computation.18 | async-start | bytes 262144 | tf_op jit(solution)/shard_map/all_to_all | solution.py:391
  367.3 19.2 %collective-permute-start.18 = (bf16[4,19,1024]{2,1,0:T(8,128)(2,1)S(1)}, bf16[4,19,1024]{2,1,0:T(8,128)(2,1)S(1)}, u32[]{:S(2)}, u32[]{:S(2)}) collective-permute-start(bf16[4,19,1024]{2,1,0:T(8,128)(2,1)S(1)} %get-tuple-element.85), channel_id=1, source_target_pairs={{0,24},{4,28},{8,0},{12,4},{16,8},{20,12},{24,16},{28,20},{1,25},{... | collective-permute-start | bytes 466952 | tf_op jit(solution)/shard_map/ppermute | solution.py:26
  370.1 16.3 %collective-permute-start.19 = (bf16[4,19,1024]{2,1,0:T(8,128)(2,1)S(1)}, bf16[4,19,1024]{2,1,0:T(8,128)(2,1)S(1)}, u32[]{:S(2)}, u32[]{:S(2)}) collective-permute-start(bf16[4,19,1024]{2,1,0:T(8,128)(2,1)S(1)} %get-tuple-element.86), channel_id=1, source_target_pairs={{0,16},{4,20},{8,24},{12,28},{16,0},{20,4},{24,8},{28,12},{1,17},{... | collective-permute-start | bytes 466952 | tf_op jit(solution)/shard_map/ppermute | solution.py:26
  370.6 15.9 %collective-permute-start.20 = (bf16[4,19,1024]{2,1,0:T(8,128)(2,1)S(1)}, bf16[4,19,1024]{2,1,0:T(8,128)(2,1)S(1)}, u32[]{:S(2)}, u32[]{:S(2)}) collective-permute-start(bf16[4,19,1024]{2,1,0:T(8,128)(2,1)S(1)} %get-tuple-element.87), channel_id=1, source_target_pairs={{0,8},{4,12},{8,16},{12,20},{16,24},{20,28},{24,0},{28,4},{1,9},{5... | collective-permute-start | bytes 466952 | tf_op jit(solution)/shard_map/ppermute | solution.py:26
  376.2 16.3 %all-to-all-start.19 = ((f32[8,8,128]{2,1,0:T(8,128)}), f32[8,8,128]{2,1,0:T(8,128)S(1)}, u32[]{:S(2)}, u32[]{:S(2)}) async-start(f32[8,8,128]{2,1,0:T(8,128)} %broadcast_in_dim.110), calls=%async_computation.19 | async-start | bytes 65536 | tf_op jit(solution)/shard_map/all_to_all | solution.py:391
  (48 other events, 768.9 us)
where the time goes:
time: 401 us; the launch traced here: 394 us
  blocking collectives  158 us (39%)
  starting transfers between devices  95.7 us (24%)
  waiting for transfers between devices  55.3 us (14%)
  local copies, waits for them, and re-layouts  44.7 us (11%)
  Pallas kernels  29.2 us (7%)
  other arithmetic  8.55 us (2%)
    all_to_all x14, blocking collectives, over_side(): lax.all_to_all(value, ('dp', 'vocab'), 0, 0, tiled=True, axis_index_group...  158 us
    ppermute x5, starting transfers between devices, other_core(): return lax.ppermute(value, 'dp', [(i, i ^ 1) for i in range(n)])  37.4 us
    ppermute x7, waiting for transfers between devices, next_section(): return lax.ppermute(value, 'section', [(i, (i + 1) % n) for i in range(n)])  26.9 us
    unnamed x88, local copies, waits for them, and re-layouts  23.2 us
    pallas_call x8, Pallas kernels, call_state(): local_call(lambda *refs: advance(section, model_width, *refs), [((sides,...  16.3 us
    all_to_all x2, starting transfers between devices, on_device(): every = lax.all_to_all(copies, axes, 0, 0, tiled=True)[:, :, :row_total]  14.2 us
    all_to_all x3, waiting for transfers between devices, over_side(): lax.all_to_all(value, ('dp', 'vocab'), 0, 0, tiled=True, axis_index_group...  13.2 us
    all_to_all x3, starting transfers between devices, over_side(): lax.all_to_all(value, ('dp', 'vocab'), 0, 0, tiled=True, axis_index_group...  11.5 us
  transfers between devices with their start and end apart: 31, of which 15 were waited for; matrix products, arithmetic and copies ran while one was open for 7% of the time, Pallas kernels for 1%

commit v1 on v0

--- a/solution.py
+++ b/solution.py
@@ -108,7 +108,8 @@
 
 
 def advance(
-    section, model_width, at_ref, sums_ref, small_ref, c1, c2, c3, x0, x1, x2, x3, w_dt, x_in, ssm_in,
+    section, model_width, at_ref, sums_ref, small_ref, c0, c1, c2, c3, x0, x1, x2, x3, w_dt, x_in,
+    ssm_in,
     mixed_ref, x_out, ssm_out, scr,
 ):
     total = sums_ref[0].astype(F32)
@@ -121,21 +122,26 @@
     scale = lax.rsqrt(squares / model_width + EPSILON)
     projected = (total[:, :wide] * scale).astype(BF16).astype(F32)
     acts = []
-    terms = jnp.zeros((rows, x0.shape[1]), F32)
-    for j, (conv, w) in enumerate(zip((small_ref, c1, c2, c3), (x0, x1, x2, x3))):
+    low = jnp.zeros((rows, x0.shape[1]), F32)
+    bc = jnp.zeros((rows, 2 * STATE_DIM), F32)
+    for j, (conv, w) in enumerate(zip((c0, c1, c2, c3), (x0, x1, x2, x3))):
         x = projected[:, j * chan : (j + 1) * chan]
         acts.append(jax.nn.silu(conv[0:rows, :] + x * conv[rows : rows + 1, :]))
-        terms = terms + jnp.dot(acts[j].astype(BF16), w[...], preferred_element_type=F32)
+        act_half = acts[j].astype(BF16)
+        low = low + jnp.dot(act_half, w[...], preferred_element_type=F32)
+        bc = bc + lax.dot_general(
+            act_half,
+            conv[PAD:, :].astype(BF16),
+            (((1,), (1,)), ((), ())),
+            preferred_element_type=F32,
+        )
     act = acts[0]
     gate = jax.nn.silu(projected[:, wide - chan :])
-    rank = w_dt.shape[0]
-    low = terms[:, :rank].astype(BF16)
-    pre = jnp.dot(low, w_dt[...], preferred_element_type=F32)
+    pre = jnp.dot(low.astype(BF16), w_dt[...], preferred_element_type=F32)
     pre = pre + small_ref[rows + 1 : rows + 2, :]
     step = jnp.maximum(pre, 0.0) + jnp.log1p(jnp.exp(-jnp.abs(pre)))
     scr[0] = step
     scr[1] = step * act
-    bc = terms[:, rank : rank + 2 * STATE_DIM]
     shape = (STATE_DIM, 2 * STATE_DIM)
     lane = lax.broadcasted_iota(jnp.int32, shape, 1)
     sub = lax.broadcasted_iota(jnp.int32, shape, 0)
@@ -265,9 +271,8 @@
     w_in = jnp.concatenate([in_own, other_core(in_own)], axis=0)
     w_out = jnp.concatenate([out_weight[0], other_core(out_weight[0])], axis=1)
 
-    w_x = jnp.concatenate([xdt_weight[0], xbc_weight[0]], axis=1)
     w_dt = dt_weight[0]
-    taps = conv_weight[0]
+    _, taps, w_x = lax.optimization_barrier((pieces, conv_weight[0], xdt_weight[0]))
     conv_old = conv_state[0]
     keep = taps.shape[0] - 1
     conv_pre = conv_bias + jnp.sum(conv_old.astype(F32) * taps[None, :keep], axis=1)
@@ -277,9 +282,9 @@
     x_kept = jnp.zeros((own_rows, chan), F32)
 
     wide = (vocab_count + 1) * chan + TAIL
-    _, w_x = lax.optimization_barrier((found, w_x))
+    conv_rows = jnp.concatenate([small[:PAD], jnp.transpose(xbc_weight[0]).astype(F32)], axis=0)
     all_x = [w_x] + [by_vocab(w_x, k) for k in range(1, vocab_count)]
-    all_conv = [by_vocab(small[:PAD], k) for k in range(1, vocab_count)]
+    all_conv = [conv_rows] + [by_vocab(conv_rows, k) for k in range(1, vocab_count)]
     call_in = local_call(
         lambda *refs: project_in(512, *refs),
         [((sides, own_rows, wide), BF16)],
@@ -297,8 +302,8 @@
             [((sides, own_rows, chan), BF16), ((own_rows, chan), F32), (ssm_now.shape, F32)],
             scratch=[(3, own_rows, chan)],
             smem=1,
-            operands=13,
-            aliases={11: 1, 12: 2},
+            operands=14,
+            aliases={12: 1, 13: 2},
             cost=pl.CostEstimate(
                 flops=10 * own_rows * chan * dt_weight.shape[1],
                 bytes_accessed=10 * chan * dt_weight.shape[1] + 8 * ssm_now.size,
@@ -321,7 +326,7 @@
     for step in range(section_count):
         (parts,) = call_in(hidden, gain, w_in)
         if step == 0:
-            _, all_x, w_out = lax.optimization_barrier((parts, all_x, w_out))
+            _, all_x, all_conv, w_out = lax.optimization_barrier((parts, all_x, all_conv, w_out))
         mixed, x_kept, ssm_now = call_state(
             step, coords, over_side(parts), small, *all_conv, *all_x, w_dt, x_kept, ssm_now
         )

time: 401 us -> 418 us (1.042)
  waiting for transfers between devices: 55.3 us -> 81.8 us
  local copies, waits for them, and re-layouts: 44.7 us -> 31.5 us
  blocking collectives: 158 us -> 170 us
  starting transfers between devices: 95.7 us -> 85.3 us
  Pallas kernels: 29.2 us -> 34.9 us
    ppermute x6, waiting for transfers between devices: 0.02 us -> 27 us  [by_vocab(): return lax.ppermute(value, 'vocab', [(i, (i + by) % n) for i in range(n)])]
    all_to_all x14, blocking collectives: 158 us -> 170 us  [over_side(): lax.all_to_all(value, ('dp', 'vocab'), 0, 0, tiled=True, axis_index_group...]
    ppermute x7, starting transfers between devices: 9.1 us -> 0.51 us  [next_section(): return lax.ppermute(value, 'section', [(i, (i + 1) % n) for i in range(n)])]
    optimization_barrier x4 -> x0, local copies, waits for them, and re-layouts: 7.82 us -> none  [the longest x3 6.76 us: on_device(): _, all_x, w_out = lax.optimization_barrier((parts, all_x, w_out))]
    pallas_call x8, Pallas kernels: 16.3 us -> 21.4 us  [call_state(): local_call(lambda *refs: advance(section, model_width, *refs), [((sides,...]
    unnamed x88 -> x59, local copies, waits for them, and re-layouts: 23.2 us -> 18.5 us
  transfers between devices with their start and end apart: 31 -> 31, of which waited for: 15 -> 16; matrix products, arithmetic and copies ran while one was open for 7% -> 4% of each run, Pallas kernels for 1% -> 1%
where the time goes in v1:
time: 418 us; the launch traced here: 413 us
  blocking collectives  170 us (41%)
  starting transfers between devices  85.3 us (20%)
  waiting for transfers between devices  81.8 us (20%)
  Pallas kernels  34.9 us (8%)
  local copies, waits for them, and re-layouts  31.5 us (8%)
  other arithmetic  6.86 us (2%)
    all_to_all x14, blocking collectives, over_side(): lax.all_to_all(value, ('dp', 'vocab'), 0, 0, tiled=True, axis_index_group...  170 us
    ppermute x5, starting transfers between devices, other_core(): return lax.ppermute(value, 'dp', [(i, i ^ 1) for i in range(n)])  35.5 us
    ppermute x7, waiting for transfers between devices, next_section(): return lax.ppermute(value, 'section', [(i, (i + 1) % n) for i in range(n)])  27.2 us
    ppermute x6, waiting for transfers between devices, by_vocab(): return lax.ppermute(value, 'vocab', [(i, (i + by) % n) for i in range(n)])  27 us
    pallas_call x8, Pallas kernels, call_state(): local_call(lambda *refs: advance(section, model_width, *refs), [((sides,...  21.4 us
    unnamed x59, local copies, waits for them, and re-layouts  18.5 us
    all_to_all x3, starting transfers between devices, over_side(): lax.all_to_all(value, ('dp', 'vocab'), 0, 0, tiled=True, axis_index_group...  13.7 us
    all_to_all x3, waiting for transfers between devices, over_side(): lax.all_to_all(value, ('dp', 'vocab'), 0, 0, tiled=True, axis_index_group...  13.2 us
  transfers between devices with their start and end apart: 31, of which 16 were waited for; matrix products, arithmetic and copies ran while one was open for 4% of the time, Pallas kernels for 1%

profile of v1, /device:TPU:1, one launch (start us, length us, event | category | flops | bytes accessed | tf_op | source)
XLA Modules:
  0.0 412.7 jit_solution(17381983787795385367)
XLA Ops:
  6.2 4.3 %copy.77 = bf16[16,8,2,4096]{3,1,2,0:T(8,128)(2,1)} copy(bf16[16,8,2,4096]{3,2,1,0:T(2,128)(2,1)} %bitcast.92) | data formatting | bytes 4194304
  14.4 6.4 %all-to-all-start = ((bf16[8,32,128]{2,1,0:T(8,128)(2,1)}), bf16[8,32,128]{2,1,0:T(8,128)(2,1)S(1)}, u32[]{:S(2)}, u32[]{:S(2)}) async-start(bf16[8,32,128]{2,1,0:T(8,128)(2,1)} %broadcast_in_dim.98), calls=%async_computation | async-start | bytes 131072 | tf_op jit(solution)/shard_map/all_to_all | solution.py:259
  39.8 6.5 %all-to-all-start.1 = ((bf16[16,4,5248]{2,1,0:T(4,128)(2,1)}), bf16[16,4,5248]{2,1,0:T(4,128)(2,1)}, u32[]{:S(2)}, u32[]{:S(2)}) async-start(bf16[16,4,5248]{2,1,0:T(4,128)(2,1)} %shard_map.212), calls=%async_computation.1 | async-start | bytes 1343488 | tf_op jit(solution)/shard_map/all_to_all | solution.py:33
  57.2 25.6 %collective-permute-done.6.refs_5_ = f32[40,1024]{1,0:T(8,128)S(1)} collective-permute-done((f32[40,1024]{1,0:T(8,128)}, f32[40,1024]{1,0:T(8,128)S(1)}, u32[]{:S(2)}, u32[]{:S(2)}) %collective-permute-start.6) | collective-permute-done | bytes 163872 | tf_op jit(solution)/shard_map/ppermute | solution.py:20
  90.4 12.8 %all_to_all.100.refs_0_ = bf16[16,4,1024]{2,1,0:T(4,128)(2,1)S(1)} all-to-all(bf16[16,4,1024]{2,1,0:T(4,128)(2,1)S(1)} %get-tuple-element.67), channel_id=1, replica_groups={{0,1,2,3,8,9,10,11,16,17,18,19,24,25,26,27},{4,5,6,7,12,13,14,15,20,21,..., dimensions={0} | all-to-all | bytes 262144 | tf_op jit(solution)/shard_map/all_to_all | solution.py:33
  109.9 13.0 %all_to_all.101.refs_1_ = bf16[16,4,5248]{2,1,0:T(4,128)(2,1)S(1)} all-to-all(bf16[16,4,5248]{2,1,0:T(4,128)(2,1)S(1)} %shard_map.215), channel_id=1, replica_groups={{0,1,2,3,8,9,10,11,16,17,18,19,24,25,26,27},{4,5,6,7,12,13,14,15,20,21,..., dimensions={0} | all-to-all | bytes 1343488 | tf_op jit(solution)/shard_map/all_to_all | solution.py:33
  125.7 9.8 %all_to_all.102.refs_0_ = bf16[16,4,1024]{2,1,0:T(4,128)(2,1)S(1)} all-to-all(bf16[16,4,1024]{2,1,0:T(4,128)(2,1)S(1)} %get-tuple-element.71), channel_id=1, replica_groups={{0,1,2,3,8,9,10,11,16,17,18,19,24,25,26,27},{4,5,6,7,12,13,14,15,20,21,..., dimensions={0} | all-to-all | bytes 262144 | tf_op jit(solution)/shard_map/all_to_all | solution.py:33
  135.9 4.1 collective-permute-done.10.refs_0_.refs_1_
  140.7 12.5 %all_to_all.103.refs_1_ = bf16[16,4,5248]{2,1,0:T(4,128)(2,1)S(1)} all-to-all(bf16[16,4,5248]{2,1,0:T(4,128)(2,1)S(1)} %shard_map.218), channel_id=1, replica_groups={{0,1,2,3,8,9,10,11,16,17,18,19,24,25,26,27},{4,5,6,7,12,13,14,15,20,21,..., dimensions={0} | all-to-all | bytes 1343488 | tf_op jit(solution)/shard_map/all_to_all | solution.py:33
  155.8 9.6 %all_to_all.104.refs_0_ = bf16[16,4,1024]{2,1,0:T(4,128)(2,1)S(1)} all-to-all(bf16[16,4,1024]{2,1,0:T(4,128)(2,1)S(1)} %get-tuple-element.74), channel_id=1, replica_groups={{0,1,2,3,8,9,10,11,16,17,18,19,24,25,26,27},{4,5,6,7,12,13,14,15,20,21,..., dimensions={0} | all-to-all | bytes 262144 | tf_op jit(solution)/shard_map/all_to_all | solution.py:33
  170.3 12.6 %all_to_all.105.refs_1_ = bf16[16,4,5248]{2,1,0:T(4,128)(2,1)S(1)} all-to-all(bf16[16,4,5248]{2,1,0:T(4,128)(2,1)S(1)} %shard_map.221), channel_id=1, replica_groups={{0,1,2,3,8,9,10,11,16,17,18,19,24,25,26,27},{4,5,6,7,12,13,14,15,20,21,..., dimensions={0} | all-to-all | bytes 1343488 | tf_op jit(solution)/shard_map/all_to_all | solution.py:33
  185.5 10.0 %all_to_all.106.refs_0_ = bf16[16,4,1024]{2,1,0:T(4,128)(2,1)S(1)} all-to-all(bf16[16,4,1024]{2,1,0:T(4,128)(2,1)S(1)} %get-tuple-element.77), channel_id=1, replica_groups={{0,1,2,3,8,9,10,11,16,17,18,19,24,25,26,27},{4,5,6,7,12,13,14,15,20,21,..., dimensions={0} | all-to-all | bytes 262144 | tf_op jit(solution)/shard_map/all_to_all | solution.py:33
  200.4 12.5 %all_to_all.107.refs_1_ = bf16[16,4,5248]{2,1,0:T(4,128)(2,1)S(1)} all-to-all(bf16[16,4,5248]{2,1,0:T(4,128)(2,1)S(1)} %shard_map.224), channel_id=1, replica_groups={{0,1,2,3,8,9,10,11,16,17,18,19,24,25,26,27},{4,5,6,7,12,13,14,15,20,21,..., dimensions={0} | all-to-all | bytes 1343488 | tf_op jit(solution)/shard_map/all_to_all | solution.py:33
  215.6 10.2 %all_to_all.108.refs_0_ = bf16[16,4,1024]{2,1,0:T(4,128)(2,1)S(1)} all-to-all(bf16[16,4,1024]{2,1,0:T(4,128)(2,1)S(1)} %get-tuple-element.80), channel_id=1, replica_groups={{0,1,2,3,8,9,10,11,16,17,18,19,24,25,26,27},{4,5,6,7,12,13,14,15,20,21,..., dimensions={0} | all-to-all | bytes 262144 | tf_op jit(solution)/shard_map/all_to_all | solution.py:33
  230.7 22.5 %all_to_all.109.refs_1_ = bf16[16,4,5248]{2,1,0:T(4,128)(2,1)S(1)} all-to-all(bf16[16,4,5248]{2,1,0:T(4,128)(2,1)S(1)} %shard_map.227), channel_id=1, replica_groups={{0,1,2,3,8,9,10,11,16,17,18,19,24,25,26,27},{4,5,6,7,12,13,14,15,20,21,..., dimensions={0} | all-to-all | bytes 1343488 | tf_op jit(solution)/shard_map/all_to_all | solution.py:33
  255.8 9.6 %all_to_all.110.refs_0_ = bf16[16,4,1024]{2,1,0:T(4,128)(2,1)S(1)} all-to-all(bf16[16,4,1024]{2,1,0:T(4,128)(2,1)S(1)} %get-tuple-element.83), channel_id=1, replica_groups={{0,1,2,3,8,9,10,11,16,17,18,19,24,25,26,27},{4,5,6,7,12,13,14,15,20,21,..., dimensions={0} | all-to-all | bytes 262144 | tf_op jit(solution)/shard_map/all_to_all | solution.py:33
  270.6 12.6 %all_to_all.111.refs_1_ = bf16[16,4,5248]{2,1,0:T(4,128)(2,1)S(1)} all-to-all(bf16[16,4,5248]{2,1,0:T(4,128)(2,1)S(1)} %shard_map.230), channel_id=1, replica_groups={{0,1,2,3,8,9,10,11,16,17,18,19,24,25,26,27},{4,5,6,7,12,13,14,15,20,21,..., dimensions={0} | all-to-all | bytes 1343488 | tf_op jit(solution)/shard_map/all_to_all | solution.py:33
  285.8 9.9 %all_to_all.112.refs_0_ = bf16[16,4,1024]{2,1,0:T(4,128)(2,1)S(1)} all-to-all(bf16[16,4,1024]{2,1,0:T(4,128)(2,1)S(1)} %get-tuple-element.86), channel_id=1, replica_groups={{0,1,2,3,8,9,10,11,16,17,18,19,24,25,26,27},{4,5,6,7,12,13,14,15,20,21,..., dimensions={0} | all-to-all | bytes 262144 | tf_op jit(solution)/shard_map/all_to_all | solution.py:33
  300.9 12.4 %all_to_all.113.refs_1_ = bf16[16,4,5248]{2,1,0:T(4,128)(2,1)S(1)} all-to-all(bf16[16,4,5248]{2,1,0:T(4,128)(2,1)S(1)} %shard_map.233), channel_id=1, replica_groups={{0,1,2,3,8,9,10,11,16,17,18,19,24,25,26,27},{4,5,6,7,12,13,14,15,20,21,..., dimensions={0} | all-to-all | bytes 1343488 | tf_op jit(solution)/shard_map/all_to_all | solution.py:33
  320.9 6.1 %all-to-all-done.16.refs_0_ = bf16[16,4,1024]{2,1,0:T(4,128)(2,1)S(1)} async-done(((bf16[16,4,1024]{2,1,0:T(4,128)(2,1)}), bf16[16,4,1024]{2,1,0:T(4,128)(2,1)S(1)}, u32[]{:S(2)}, u32[]{:S(2)}) %all-to-all-start.16) | async-done | bytes 131104 | tf_op jit(solution)/shard_map/all_to_all | solution.py:33
  340.6 7.1 %all-to-all-done.17 = bf16[16,16,384]{2,1,0:T(8,128)(2,1)S(1)} async-done(((bf16[16,16,384]{2,1,0:T(8,128)(2,1)}), bf16[16,16,384]{2,1,0:T(8,128)(2,1)S(1)}, u32[]{:S(2)}, u32[]{:S(2)}) %all-to-all-start.17) | async-done | bytes 196640 | tf_op jit(solution)/shard_map/all_to_all | solution.py:33
  347.7 30.2 %collective-permute-start.24 = (bf16[16,16,384]{2,1,0:T(8,128)(2,1)S(1)}, bf16[16,16,384]{2,1,0:T(8,128)(2,1)S(1)}, u32[]{:S(2)}, u32[]{:S(2)}) collective-permute-start(bf16[16,16,384]{2,1,0:T(8,128)(2,1)S(1)} %all-to-all-done.17), channel_id=1, source_target_pairs={{0,4},{4,0},{8,12},{12,8},{16,20},{20,16},{24,28},{28,24},{1,5},{5... | collective-permute-start | bytes 589832 | tf_op jit(solution)/shard_map/ppermute | solution.py:38
  395.0 9.3 %all-to-all-start.19 = ((f32[8,8,128]{2,1,0:T(8,128)}), f32[8,8,128]{2,1,0:T(8,128)S(1)}, u32[]{:S(2)}, u32[]{:S(2)}) async-start(f32[8,8,128]{2,1,0:T(8,128)} %broadcast_in_dim.110), calls=%async_computation.19 | async-start | bytes 65536 | tf_op jit(solution)/shard_map/all_to_all | solution.py:396
  407.0 4.2 %all-to-all-done.19 = f32[8,8,128]{2,1,0:T(8,128)S(1)} async-done(((f32[8,8,128]{2,1,0:T(8,128)}), f32[8,8,128]{2,1,0:T(8,128)S(1)}, u32[]{:S(2)}, u32[]{:S(2)}) %all-to-all-start.19) | async-done | bytes 32800 | tf_op jit(solution)/shard_map/all_to_all | solution.py:396
  (205 shorter events, 137.3 us)
Async XLA Ops:
  10.5 22.4 %collective-permute-start.1 = (bf16[128,8192]{1,0:T(8,128)(2,1)}, bf16[128,8192]{1,0:T(8,128)(2,1)}, u32[]{:S(2)}, u32[]{:S(2)}) collective-permute-start(bf16[128,8192]{1,0:T(8,128)(2,1)} %bitcast.48), channel_id=1, source_target_pairs={{0,4},{4,0},{8,12},{12,8},{16,20},{20,16},{24,28},{28,24},{1,5},{5... | collective-permute-start | bytes 6291464 | tf_op jit(solution)/shard_map/ppermute | solution.py:38
  14.4 13.6 %all-to-all-start = ((bf16[8,32,128]{2,1,0:T(8,128)(2,1)}), bf16[8,32,128]{2,1,0:T(8,128)(2,1)S(1)}, u32[]{:S(2)}, u32[]{:S(2)}) async-start(bf16[8,32,128]{2,1,0:T(8,128)(2,1)} %broadcast_in_dim.98), calls=%async_computation | async-start | bytes 131072 | tf_op jit(solution)/shard_map/all_to_all | solution.py:259
  20.8 30.7 %collective-permute-start.8 = (bf16[4096,128]{1,0:T(8,128)(2,1)}, bf16[4096,128]{1,0:T(8,128)(2,1)}, u32[]{:S(2)}, u32[]{:S(2)}) collective-permute-start(bf16[4096,128]{1,0:T(8,128)(2,1)} %bitcast.16), channel_id=1, source_target_pairs={{0,4},{4,0},{8,12},{12,8},{16,20},{20,16},{24,28},{28,24},{1,5},{5... | collective-permute-start | bytes 3145736 | tf_op jit(solution)/shard_map/ppermute | solution.py:38
  28.0 4.3 %collective-permute-start = (f32[9,4,128]{2,1,0:T(4,128)S(1)}, f32[9,4,128]{2,1,0:T(4,128)S(1)}, u32[]{:S(2)}, u32[]{:S(2)}) collective-permute-start(f32[9,4,128]{2,1,0:T(4,128)S(1)} %pad_maximum_fusion.2.refs_1_), channel_id=1, source_target_pairs={{0,4},{4,0},{8,12},{12,8},{16,20},{20,16},{24,28},{28,24},{1,5},{5... | collective-permute-start | bytes 55304 | tf_op jit(solution)/shard_map/ppermute | solution.py:38
  31.1 20.2 %collective-permute-start.5 = (f32[40,1024]{1,0:T(8,128)}, f32[40,1024]{1,0:T(8,128)}, u32[]{:S(2)}, u32[]{:S(2)}) collective-permute-start(f32[40,1024]{1,0:T(8,128)} %concatenate.25.refs_3_), channel_id=1, source_target_pairs={{0,1},{1,2},{2,3},{3,0},{4,5},{5,6},{6,7},{7,4},{8,9},{9,10},{10,1... | collective-permute-start | bytes 491528 | tf_op jit(solution)/shard_map/ppermute | solution.py:20
  39.8 45.8 %all-to-all-start.1 = ((bf16[16,4,5248]{2,1,0:T(4,128)(2,1)}), bf16[16,4,5248]{2,1,0:T(4,128)(2,1)}, u32[]{:S(2)}, u32[]{:S(2)}) async-start(bf16[16,4,5248]{2,1,0:T(4,128)(2,1)} %shard_map.212), calls=%async_computation.1 | async-start | bytes 1343488 | tf_op jit(solution)/shard_map/all_to_all | solution.py:33
  46.3 39.3 %collective-permute-start.2 = (bf16[1024,256]{1,0:T(8,128)(2,1)S(1)}, bf16[1024,256]{1,0:T(8,128)(2,1)}, u32[]{:S(2)}, u32[]{:S(2)}) collective-permute-start(bf16[1024,256]{1,0:T(8,128)(2,1)S(1)} %bitcast.69), channel_id=1, source_target_pairs={{0,1},{1,2},{2,3},{3,0},{4,5},{5,6},{6,7},{7,4},{8,9},{9,10},{10,1... | collective-permute-start | bytes 1572872 | tf_op jit(solution)/shard_map/ppermute | solution.py:20
  47.7 37.9 %collective-permute-start.3 = (bf16[1024,256]{1,0:T(8,128)(2,1)S(1)}, bf16[1024,256]{1,0:T(8,128)(2,1)}, u32[]{:S(2)}, u32[]{:S(2)}) collective-permute-start(bf16[1024,256]{1,0:T(8,128)(2,1)S(1)} %bitcast.70), channel_id=1, source_target_pairs={{0,2},{1,3},{2,0},{3,1},{4,6},{5,7},{6,4},{7,5},{8,10},{9,11},{10,... | collective-permute-start | bytes 1572872 | tf_op jit(solution)/shard_map/ppermute | solution.py:20
  50.1 35.5 %collective-permute-start.4 = (bf16[1024,256]{1,0:T(8,128)(2,1)S(1)}, bf16[1024,256]{1,0:T(8,128)(2,1)}, u32[]{:S(2)}, u32[]{:S(2)}) collective-permute-start(bf16[1024,256]{1,0:T(8,128)(2,1)S(1)} %bitcast.71), channel_id=1, source_target_pairs={{0,3},{1,0},{2,1},{3,2},{4,7},{5,4},{6,5},{7,6},{8,11},{9,8},{10,9... | collective-permute-start | bytes 1572872 | tf_op jit(solution)/shard_map/ppermute | solution.py:20
  51.3 31.4 %collective-permute-start.6 = (f32[40,1024]{1,0:T(8,128)}, f32[40,1024]{1,0:T(8,128)S(1)}, u32[]{:S(2)}, u32[]{:S(2)}) collective-permute-start(f32[40,1024]{1,0:T(8,128)} %concatenate.25.refs_3_), channel_id=1, source_target_pairs={{0,2},{1,3},{2,0},{3,1},{4,6},{5,7},{6,4},{7,5},{8,10},{9,11},{10,... | collective-permute-start | bytes 491528 | tf_op jit(solution)/shard_map/ppermute | solution.py:20
  51.6 33.3 %collective-permute-start.7 = (f32[40,1024]{1,0:T(8,128)}, f32[40,1024]{1,0:T(8,128)S(1)}, u32[]{:S(2)}, u32[]{:S(2)}) collective-permute-start(f32[40,1024]{1,0:T(8,128)} %concatenate.25.refs_3_), channel_id=1, source_target_pairs={{0,3},{1,0},{2,1},{3,2},{4,7},{5,4},{6,5},{7,6},{8,11},{9,8},{10,9... | collective-permute-start | bytes 491528 | tf_op jit(solution)/shard_map/ppermute | solution.py:20
  135.9 4.1 collective-permute-start.10
  265.8 4.1 collective-permute-start.14
  316.6 10.5 %all-to-all-start.16 = ((bf16[16,4,1024]{2,1,0:T(4,128)(2,1)}), bf16[16,4,1024]{2,1,0:T(4,128)(2,1)S(1)}, u32[]{:S(2)}, u32[]{:S(2)}) async-start(bf16[16,4,1024]{2,1,0:T(4,128)(2,1)} %copy-done.13), calls=%async_computation.16 | async-start | bytes 262144 | tf_op jit(solution)/shard_map/all_to_all | solution.py:33
  330.4 5.9 %collective-permute-start.21 = (bf16[16,384]{1,0:T(8,128)(2,1)S(1)}, bf16[16,384]{1,0:T(8,128)(2,1)S(1)}, u32[]{:S(2)}, u32[]{:S(2)}) collective-permute-start(bf16[16,384]{1,0:T(8,128)(2,1)S(1)} %broadcast_select_fusion), channel_id=1, source_target_pairs={{224,0},{96,128},{225,1},{97,129},{226,2},{98,130},{227,3},{99,131... | collective-permute-start | bytes 36872 | tf_op jit(solution)/shard_map/ppermute | solution.py:353
  331.7 4.6 %collective-permute-start.22 = (bf16[16,384]{1,0:T(8,128)(2,1)S(1)}, bf16[16,384]{1,0:T(8,128)(2,1)S(1)}, u32[]{:S(2)}, u32[]{:S(2)}) collective-permute-start(bf16[16,384]{1,0:T(8,128)(2,1)S(1)} %broadcast_select_fusion), channel_id=1, source_target_pairs={{224,32},{96,160},{225,33},{97,161},{226,34},{98,162},{227,35},{99... | collective-permute-start | bytes 36872 | tf_op jit(solution)/shard_map/ppermute | solution.py:353
  337.0 10.7 %all-to-all-start.17 = ((bf16[16,16,384]{2,1,0:T(8,128)(2,1)}), bf16[16,16,384]{2,1,0:T(8,128)(2,1)S(1)}, u32[]{:S(2)}, u32[]{:S(2)}) async-start(bf16[16,16,384]{2,1,0:T(8,128)(2,1)} %broadcast_in_dim.105), calls=%async_computation.17 | async-start | bytes 393216 | tf_op jit(solution)/shard_map/all_to_all | solution.py:33
  347.7 31.3 %collective-permute-start.24 = (bf16[16,16,384]{2,1,0:T(8,128)(2,1)S(1)}, bf16[16,16,384]{2,1,0:T(8,128)(2,1)S(1)}, u32[]{:S(2)}, u32[]{:S(2)}) collective-permute-start(bf16[16,16,384]{2,1,0:T(8,128)(2,1)S(1)} %all-to-all-done.17), channel_id=1, source_target_pairs={{0,4},{4,0},{8,12},{12,8},{16,20},{20,16},{24,28},{28,24},{1,5},{5... | collective-permute-start | bytes 589832 | tf_op jit(solution)/shard_map/ppermute | solution.py:38
  378.0 8.5 %collective-permute-start.17 = (bf16[4,19,1024]{2,1,0:T(8,128)(2,1)S(1)}, bf16[4,19,1024]{2,1,0:T(8,128)(2,1)S(1)}, u32[]{:S(2)}, u32[]{:S(2)}) collective-permute-start(bf16[4,19,1024]{2,1,0:T(8,128)(2,1)S(1)} %pad_maximum_fusion.1.own_ref), channel_id=1, source_target_pairs={{0,4},{4,0},{8,12},{12,8},{16,20},{20,16},{24,28},{28,24},{1,5},{5... | collective-permute-start | bytes 466952 | tf_op jit(solution)/shard_map/ppermute | solution.py:38
  382.6 11.6 %all-to-all-start.18 = ((f32[32,8,128]{2,1,0:T(8,128)}), f32[32,8,128]{2,1,0:T(8,128)S(1)}, u32[]{:S(2)}, u32[]{:S(2)}) async-start(f32[32,8,128]{2,1,0:T(8,128)} %broadcast_in_dim.109), calls=%async_computation.18 | async-start | bytes 262144 | tf_op jit(solution)/shard_map/all_to_all | solution.py:396
  387.9 17.1 %collective-permute-start.18 = (bf16[4,19,1024]{2,1,0:T(8,128)(2,1)}, bf16[4,19,1024]{2,1,0:T(8,128)(2,1)S(1)}, u32[]{:S(2)}, u32[]{:S(2)}) collective-permute-start(bf16[4,19,1024]{2,1,0:T(8,128)(2,1)} %get-tuple-element.95), channel_id=1, source_target_pairs={{0,24},{4,28},{8,0},{12,4},{16,8},{20,12},{24,16},{28,20},{1,25},{... | collective-permute-start | bytes 466952 | tf_op jit(solution)/shard_map/ppermute | solution.py:26
  390.7 14.4 %collective-permute-start.19 = (bf16[4,19,1024]{2,1,0:T(8,128)(2,1)S(1)}, bf16[4,19,1024]{2,1,0:T(8,128)(2,1)S(1)}, u32[]{:S(2)}, u32[]{:S(2)}) collective-permute-start(bf16[4,19,1024]{2,1,0:T(8,128)(2,1)S(1)} %get-tuple-element.96), channel_id=1, source_target_pairs={{0,16},{4,20},{8,24},{12,28},{16,0},{20,4},{24,8},{28,12},{1,17},{... | collective-permute-start | bytes 466952 | tf_op jit(solution)/shard_map/ppermute | solution.py:26
  391.1 13.9 %collective-permute-start.20 = (bf16[4,19,1024]{2,1,0:T(8,128)(2,1)S(1)}, bf16[4,19,1024]{2,1,0:T(8,128)(2,1)S(1)}, u32[]{:S(2)}, u32[]{:S(2)}) collective-permute-start(bf16[4,19,1024]{2,1,0:T(8,128)(2,1)S(1)} %get-tuple-element.97), channel_id=1, source_target_pairs={{0,8},{4,12},{8,16},{12,20},{16,24},{20,28},{24,0},{28,4},{1,9},{5... | collective-permute-start | bytes 466952 | tf_op jit(solution)/shard_map/ppermute | solution.py:26
  395.0 16.2 %all-to-all-start.19 = ((f32[8,8,128]{2,1,0:T(8,128)}), f32[8,8,128]{2,1,0:T(8,128)S(1)}, u32[]{:S(2)}, u32[]{:S(2)}) async-start(f32[8,8,128]{2,1,0:T(8,128)} %broadcast_in_dim.110), calls=%async_computation.19 | async-start | bytes 65536 | tf_op jit(solution)/shard_map/all_to_all | solution.py:396
  (34 other events, 643.1 us)
